TPU v7x, 512 devices: a whole 4x8x8 slice. The times are simulated.
512 devices in a mesh: clip: 32 (over x, z), seq: 8 (over y), tp: 2 (over core).
Axes of the slice: x: 4, y: 8, z: 8, core: 2. Of those that a mesh axis runs over, the one named last changes fastest.
Arguments:
- projections: bfloat16 [65536, 32, 384], P(('clip', 'seq', 'tp')), parts along dimension 0, may hold values from -64 to 64
- tile_mask: int32 [1024, 16, 16], P('clip'), parts along dimension 0, may hold values from 0 to 1, as said below
Outputs:
- attention: bfloat16 [65536, 4096], P(('clip', 'seq', 'tp')), parts along dimension 0
There are 32 independent parts, one for each index of `clip`. A program takes and returns all parts, laid end to end along the dimension named above; each array names one. Nothing has to cross between parts.
Inputs may be any that keep to these rules, and one draw needn't show every extreme that they name: tile_mask[h, a, a] = 1 for every head h and tile a.
All inputs are finite; a program needn't handle non-finite values.
Results may differ from a plain program's by a relative error of at most 0.0055.
Values may be sent and summed in bfloat16 or wider, within the bound.
A program may use at most 64 MiB of HBM per device.

v0:
```python
import math

import jax
import jax.numpy as jnp
from jax import lax
from jax.sharding import PartitionSpec as P

TILE = 128
SPAN = 512


NEGATIVE_FILL = -1e30


def block_activity(tile_mask, per_block):
    head_count, tile_count, _ = tile_mask.shape
    block_count = tile_count // per_block
    grouped = tile_mask.reshape(head_count, block_count, per_block, block_count, per_block)
    return (
        (jnp.sum(grouped, axis=(2, 4)) > 0)
        .astype(jnp.int32)
        .reshape(head_count, block_count * block_count)
    )


def head_attention(slot_data, head_tiles, head_active, tile_rows, block_rows):
    seq_length, row_width = slot_data.shape
    head_dim = row_width // 3
    block_count = seq_length // block_rows
    per_block = block_rows // tile_rows
    pair_total = block_count * block_count
    pair_order = jnp.argsort(
        (1 - head_active) * pair_total + jnp.arange(pair_total, dtype=jnp.int32), stable=True
    )
    active_count = jnp.sum(head_active)
    score_scale = 1.0 / math.sqrt(head_dim)

    def advance(turn_index, carried):
        row_max, row_sum, weighted = carried
        pair_index = pair_order[turn_index]
        query_start = pair_index // block_count * block_rows
        key_start = pair_index % block_count * block_rows
        queries = lax.dynamic_slice(slot_data, (query_start, 0), (block_rows, head_dim))
        key_values = lax.dynamic_slice(slot_data, (key_start, head_dim), (block_rows, 2 * head_dim))
        scores = (
            lax.dot_general(
                queries,
                key_values[:, :head_dim],
                (((1,), (1,)), ((), ())),
                preferred_element_type=jnp.float32,
            )
            * score_scale
        )
        tile_block = lax.dynamic_slice(
            head_tiles, (query_start // tile_rows, key_start // tile_rows), (per_block, per_block)
        )
        allowed = jnp.broadcast_to(
            tile_block[:, None, :, None] > 0, (per_block, tile_rows, per_block, tile_rows)
        ).reshape(block_rows, block_rows)
        masked = jnp.where(allowed, scores, NEGATIVE_FILL)
        old_max = lax.dynamic_slice_in_dim(row_max, query_start, block_rows)
        new_max = jnp.maximum(old_max, jnp.max(masked, axis=1))
        expo = jnp.where(allowed, jnp.exp(masked - new_max[:, None]), 0.0)
        factor = jnp.exp(old_max - new_max)
        old_sum = lax.dynamic_slice_in_dim(row_sum, query_start, block_rows)
        old_weighted = lax.dynamic_slice_in_dim(weighted, query_start, block_rows)
        product = jnp.dot(
            expo.astype(jnp.bfloat16), key_values[:, head_dim:], preferred_element_type=jnp.float32
        )
        row_max = lax.dynamic_update_slice_in_dim(row_max, new_max, query_start, 0)
        row_sum = lax.dynamic_update_slice_in_dim(
            row_sum, old_sum * factor + jnp.sum(expo, axis=1), query_start, 0
        )
        weighted = lax.dynamic_update_slice_in_dim(
            weighted, old_weighted * factor[:, None] + product, query_start, 0
        )
        return (row_max, row_sum, weighted)

    start_state = (
        jnp.full((seq_length,), NEGATIVE_FILL, jnp.float32),
        jnp.zeros((seq_length,), jnp.float32),
        jnp.zeros((seq_length, head_dim), jnp.float32),
    )
    row_max, row_sum, weighted = lax.fori_loop(0, active_count, advance, start_state)
    divisor = jnp.where(row_sum > 0.0, row_sum, 1.0)
    return (weighted / divisor[:, None]).astype(jnp.bfloat16)


def body(projections, tile_mask):
    local_rows, head_count, row_width = projections.shape
    head_dim = row_width // 3
    owner_count = lax.axis_size(("seq", "tp"))
    device_index = lax.axis_index(("seq", "tp"))
    slot_count = (head_count + owner_count - 1) // owner_count
    seq_length = local_rows * owner_count
    activity = block_activity(tile_mask, SPAN // TILE)
    head_ids = jnp.arange(head_count, dtype=jnp.int32)
    owner = head_ids % owner_count
    slot_of = head_ids // owner_count
    device_ids = jnp.arange(owner_count, dtype=jnp.int32)
    slot_ids = jnp.arange(slot_count, dtype=jnp.int32)
    chosen = (owner[None, None, :] == device_ids[:, None, None]) & (
        slot_of[None, None, :] == slot_ids[None, :, None]
    )
    selector = chosen.astype(jnp.bfloat16)
    outgoing = jnp.einsum(
        "gjh,rhc->gjrc", selector, projections, preferred_element_type=jnp.float32
    ).astype(jnp.bfloat16)
    joined = outgoing.reshape(owner_count, slot_count, 1, local_rows, row_width)
    arrived = lax.all_to_all(joined, ("seq", "tp"), split_axis=0, concat_axis=2, tiled=True)
    arrived = arrived.reshape(slot_count, seq_length, row_width)
    mine = lax.dynamic_index_in_dim(chosen, device_index, 0, keepdims=False).astype(jnp.int32)
    my_heads = jnp.sum(mine * head_ids[None, :], axis=1)
    occupied = jnp.sum(mine, axis=1)
    results = []
    for slot_index in range(slot_count):
        head_tiles = (
            lax.dynamic_index_in_dim(tile_mask, my_heads[slot_index], 0, keepdims=False)
            * occupied[slot_index]
        )
        head_active = (
            lax.dynamic_index_in_dim(activity, my_heads[slot_index], 0, keepdims=False)
            * occupied[slot_index]
        )
        results.append(head_attention(arrived[slot_index], head_tiles, head_active, TILE, SPAN))
    finished = jnp.stack(results).reshape(1, slot_count, owner_count, local_rows, head_dim)
    returned = lax.all_to_all(finished, ("seq", "tp"), split_axis=2, concat_axis=0, tiled=True)
    returned = returned.reshape(owner_count, slot_count, local_rows, head_dim)
    placed = jnp.einsum(
        "gjh,gjrc->rhc", selector, returned, preferred_element_type=jnp.float32
    ).astype(jnp.bfloat16)
    return placed.reshape(local_rows, head_count * head_dim)


def solution(mesh):
    return jax.shard_map(
        body,
        mesh=mesh,
        in_specs=(P(("clip", "seq", "tp"), None, None), P("clip", None, None)),
        out_specs=P(("clip", "seq", "tp"), None),
        check_vma=False,
    )
```

profile of v0, /device:TPU:1, one launch (start us, length us, event | category | flops | bytes accessed | tf_op | source)
XLA Modules:
  0.0 433.9 jit_solution(6291425770488095539)
XLA Ops:
  0.1 1.8 copy-done
  2.9 2.5 copy.25
  5.3 11.2 %all-to-all-start = ((bf16[16,2,1,128,384]{4,3,1,2,0:T(8,128)(2,1)}), bf16[16,2,1,128,384]{4,3,1,2,0:T(8,128)(2,1)}, u32[]{:S(2)}, u32[]{:S(2)}) async-start(bf16[16,2,1,128,384]{4,3,1,2,0:T(8,128)(2,1)} %copy.25), calls=%async_computation | async-start | bytes 6291456 | tf_op jit(solution)/shard_map/all_to_all | solution.py:110
  22.0 1.3 fusion.45
  23.3 2.1 multiply_reduce_fusion.1
  29.1 58.6 %all-to-all-done = bf16[16,2,1,128,384]{4,3,1,2,0:T(8,128)(2,1)} async-done(((bf16[16,2,1,128,384]{4,3,1,2,0:T(8,128)(2,1)}), bf16[16,2,1,128,384]{4,3,1,2,0:T(8,128)(2,1)}, u32[]{:S(2)}, u32[]{:S(2)}) %all-to-all-start) | async-done | bytes 3145760 | tf_op jit(solution)/shard_map/all_to_all | solution.py:110
  87.7 2.4 copy.66
  90.1 2.2 fusion.43
  93.3 152.3 %while.34 = (s32[]{:T(128)}, f32[2048]{0:T(1024)S(1)}, f32[2048]{0:T(1024)S(1)}, f32[2048,128]{1,0:T(8,128)}, s32[]{:T(128)}, /*index=5*/s32[16]{0:T(128)S(1)}, ...) while((s32[]{:T(128)}, f32[2048]{0:T(1024)S(1)}, ...), condition=%wide.region_8.9_spmd, body=%wide.region_5.8_spmd.sunk | while | flops 136709200 | bytes 9370636 | solution.py:84
  97.6 1.3 fusion.61
  100.3 2.5 fusion.64
  107.1 1.3 fusion.61
  109.8 2.5 fusion.64
  116.5 1.3 fusion.61
  119.3 2.5 fusion.64
  126.0 1.3 fusion.61
  128.8 2.5 fusion.64
  135.5 1.3 fusion.61
  138.3 2.5 fusion.64
  145.0 1.3 fusion.61
  147.8 2.5 fusion.64
  154.5 1.3 fusion.61
  157.3 2.5 fusion.64
  164.0 1.3 fusion.61
  166.8 2.5 fusion.64
  173.5 1.3 fusion.61
  176.2 2.5 fusion.64
  183.0 1.3 fusion.61
  185.7 2.5 fusion.64
  192.4 1.3 fusion.61
  195.2 2.5 fusion.64
  201.9 1.3 fusion.61
  204.7 2.5 fusion.64
  211.4 1.3 fusion.61
  214.1 2.5 fusion.64
  220.8 1.3 fusion.61
  223.6 2.5 fusion.64
  230.3 1.3 fusion.61
  233.1 2.5 fusion.64
  242.6 2.5 fusion.64
  246.7 139.6 %while.35 = (s32[]{:T(128)}, f32[2048]{0:T(1024)S(1)}, f32[2048]{0:T(1024)S(1)}, f32[2048,128]{1,0:T(8,128)}, s32[]{:T(128)}, /*index=5*/s32[16]{0:T(128)S(1)}, ...) while((s32[]{:T(128)}, f32[2048]{0:T(1024)S(1)}, ...), condition=%wide.region_14.15_spmd, body=%wide.region_11.14_spmd.sunk | while | flops 136709200 | bytes 9370636 | solution.py:84
  250.8 1.3 fusion.67
  253.5 2.5 fusion.70
  260.0 1.3 fusion.67
  262.8 2.5 fusion.70
  272.1 2.5 fusion.70
  278.6 1.3 fusion.67
  281.3 2.5 fusion.70
  290.6 2.5 fusion.70
  297.1 1.3 fusion.67
  299.9 2.5 fusion.70
  309.2 2.5 fusion.70
  315.7 1.3 fusion.67
  318.4 2.5 fusion.70
  327.7 2.5 fusion.70
  337.0 2.5 fusion.70
  346.2 2.5 fusion.70
  355.5 2.5 fusion.70
  364.8 2.5 fusion.70
  374.0 2.5 fusion.70
  383.3 2.5 fusion.70
  386.4 1.7 divide_convert_fusion.1
  389.6 42.1 %all_to_all.30 = bf16[1,2,16,128,128]{4,1,3,0,2:T(2,128)(2,1)S(1)} all-to-all(bf16[1,2,16,128,128]{4,1,3,0,2:T(2,128)(2,1)S(1)} %copy.28), channel_id=1, replica_groups=mesh['clip'=32,'seq'=8,'tp'=2] {'seq','tp'}, dimensions={2} | all-to-all | bytes 2097152 | tf_op jit(solution)/shard_map/all_to_all | solution.py:127
  432.5 1.4 copy.67
  (359 shorter events, 97.0 us)
Async XLA Ops:
  0.0 1.9 copy-start
  5.3 16.1 %copy-start.4 = (s32[32,16,16]{0,2,1:T(8,128)S(1)}, s32[32,16,16]{0,2,1:T(8,128)}, u32[]{:S(2)}) copy-start(s32[32,16,16]{0,2,1:T(8,128)} %param.7) | copy-start | bytes 98308
  5.3 82.4 %all-to-all-start = ((bf16[16,2,1,128,384]{4,3,1,2,0:T(8,128)(2,1)}), bf16[16,2,1,128,384]{4,3,1,2,0:T(8,128)(2,1)}, u32[]{:S(2)}, u32[]{:S(2)}) async-start(bf16[16,2,1,128,384]{4,3,1,2,0:T(8,128)(2,1)} %copy.25), calls=%async_computation | async-start | bytes 6291456 | tf_op jit(solution)/shard_map/all_to_all | solution.py:110
  98.9 1.0 copy-start.1
  108.4 1.0 copy-start.1
  117.9 1.0 copy-start.1
  127.4 1.0 copy-start.1
  136.9 1.0 copy-start.1
  146.4 1.0 copy-start.1
  155.8 1.0 copy-start.1
  165.3 1.0 copy-start.1
  174.8 1.0 copy-start.1
  184.3 1.0 copy-start.1
  193.7 1.0 copy-start.1
  203.2 1.0 copy-start.1
  212.7 1.0 copy-start.1
  222.2 1.0 copy-start.1
  231.6 1.0 copy-start.1
  241.1 1.0 copy-start.1
  252.1 1.0 copy-start.2
  261.4 1.0 copy-start.2
  270.6 1.0 copy-start.2
  279.9 1.0 copy-start.2
  289.2 1.0 copy-start.2
  298.5 1.0 copy-start.2
  307.7 1.0 copy-start.2
  317.0 1.0 copy-start.2
  326.3 1.0 copy-start.2
  335.5 1.0 copy-start.2
  344.8 1.0 copy-start.2
  354.1 1.0 copy-start.2
  363.3 1.0 copy-start.2
  372.6 1.0 copy-start.2
  381.9 1.0 copy-start.2
  386.3 1.7 copy-start.3
where the time goes:
time: 437 us; the launch traced here: 434 us
  matrix products  120 us (27%)
  loops' own time  102 us (23%)
  local copies, waits for them, and re-layouts  64.6 us (15%)
  waiting for transfers between devices  58.6 us (13%)
  blocking collectives  42.1 us (10%)
  other arithmetic  31.5 us (7%)
  starting transfers between devices  11.2 us (3%)
    another operation x2, loops' own time, head_attention(): lax.fori_loop(0, active_count, advance, start_state)  102 us
    dot_general x31, matrix products, advance(): jnp.dot(expo.astype(jnp.bfloat16), key_values[:, head_dim:], preferred_el...  77 us
    all_to_all x1, waiting for transfers between devices, body(): lax.all_to_all(joined, ('seq', 'tp'), split_axis=0, concat_axis=2, tiled=...  58.6 us
    all_to_all x1, blocking collectives, body(): lax.all_to_all(finished, ('seq', 'tp'), split_axis=2, concat_axis=0, tile...  42.1 us
    dot_general x31, matrix products, advance(): lax.dot_general(queries, key_values[:, :head_dim], (((1,), (1,)), ((), ()...  41 us
    while x124, local copies, waits for them, and re-layouts  23.6 us
    dynamic_slice x31, local copies, waits for them, and re-layouts, advance(): pair_index = pair_order[turn_index]  18.6 us
    all_to_all x1, starting transfers between devices, body(): lax.all_to_all(joined, ('seq', 'tp'), split_axis=0, concat_axis=2, tiled=...  11.2 us
  transfers between devices with their start and end apart: 1, of which 1 were waited for; matrix products, arithmetic and copies ran while one was open for 2% of the time, Pallas kernels for 0%

commit v1 on v0

v1 whole, which is shorter than its diff:
```python
import functools
import math

import jax
import jax.numpy as jnp
from jax import lax
from jax.experimental import pallas as pl
from jax.experimental.pallas import tpu as pltpu
from jax.sharding import PartitionSpec as P

MESH = pl.DeviceIdType.MESH
NEGATIVE_FILL = -1e30
CHIPS = 8
CORES = 2
PEERS = CHIPS * CORES
REACH = (1, 7, 2, 6, 3, 5, 4)
OFFSETS = tuple((d, f) for d in REACH for f in range(CORES)) + ((0, 1),)


def kernel(
    x_ref,
    mask_ref,
    out_ref,
    x_in,
    mask_in,
    kv_out,
    q_out,
    kv_got,
    q_got,
    o_out,
    tile_of_key,
    bias,
    scores,
    in_sem,
    mask_sem,
    own_sem,
    send_sem,
    recv_sem,
):
    y = lax.axis_index("seq")
    core = lax.axis_index("tp")
    me = y * CORES + core
    tokens, _, width = x_ref.shape
    slots = x_in.shape[0]
    dim = width // 3
    pair = CORES * tokens
    keys = kv_got.shape[1]

    for slot in range(slots):
        pltpu.make_async_copy(
            x_ref.at[:, pl.ds(slot * PEERS, PEERS), :], x_in.at[slot], in_sem.at[slot]
        ).start()
        pltpu.make_async_copy(
            mask_ref.at[slot * PEERS + me], mask_in.at[slot], mask_sem.at[slot]
        ).start()

    def peer(d, f):
        return {"seq": lax.rem(y + d, CHIPS), "tp": lax.rem(core + f, CORES)}

    def index_of(d, f):
        return lax.rem(y + d, CHIPS) * CORES + lax.rem(core + f, CORES)

    barrier = pltpu.get_barrier_semaphore()
    for d, f in OFFSETS:
        pl.semaphore_signal(barrier, inc=1, device_id=peer(d, f), device_id_type=MESH)

    def rows_of(device):
        return pl.ds(pl.multiple_of(device * tokens, tokens), tokens)

    def remote(kind, slot, d, f):
        to = index_of(d, f)
        if kind == "kv":
            src, dst, row = kv_out.at[slot, to], kv_got.at[slot, rows_of(me)], slot
        elif kind == "q":
            src, dst, row = q_out.at[slot, to], q_got.at[slot, rows_of(me)], 2 + slot
        else:
            columns = pl.ds(pl.multiple_of((slot * PEERS + me) * dim, dim), dim)
            src, dst, row = o_out.at[slot, rows_of(to)], out_ref.at[:, columns], 4 + slot
        number = d * CORES + f
        return pltpu.make_async_remote_copy(
            src_ref=src,
            dst_ref=dst,
            send_sem=send_sem.at[row, number],
            recv_sem=recv_sem.at[row, number],
            device_id=peer(d, f),
            device_id_type=MESH,
        )

    def own(kind, slot):
        if kind == "kv":
            src, dst, row = kv_out.at[slot, me], kv_got.at[slot, rows_of(me)], slot
        elif kind == "q":
            src, dst, row = q_out.at[slot, me], q_got.at[slot, rows_of(me)], 2 + slot
        else:
            columns = pl.ds(pl.multiple_of((slot * PEERS + me) * dim, dim), dim)
            src, dst, row = o_out.at[slot, rows_of(me)], out_ref.at[:, columns], 4 + slot
        return pltpu.make_async_copy(src, dst, own_sem.at[row])

    tile_of_key[...] = (
        lax.broadcasted_iota(jnp.int32, tile_of_key.shape, 0) // tokens
        == lax.broadcasted_iota(jnp.int32, tile_of_key.shape, 1)
    ).astype(jnp.bfloat16)
    bias[...] = jnp.zeros_like(bias)
    for slot in range(slots):
        pltpu.make_async_copy(
            mask_ref.at[slot * PEERS + me], mask_in.at[slot], mask_sem.at[slot]
        ).wait()
        bias[slot, :, 0:PEERS] = jnp.where(mask_in[slot] > 0, 0.0, NEGATIVE_FILL)

    side = PEERS * PEERS
    to_row = lax.broadcasted_iota(jnp.int32, (side, side), 0)
    from_row = lax.broadcasted_iota(jnp.int32, (side, side), 1)
    swap = (from_row == (to_row % PEERS) * PEERS + to_row // PEERS).astype(jnp.bfloat16)

    def regroup(slot, columns, target):
        for start in range(0, tokens, PEERS):
            block = x_in[slot, start : start + PEERS, :, columns].reshape(side, -1)
            swapped = jnp.dot(swap, block, preferred_element_type=jnp.float32)
            target[slot, :, start : start + PEERS, :] = swapped.astype(jnp.bfloat16).reshape(
                PEERS, PEERS, -1
            )

    for slot in range(slots):
        pltpu.make_async_copy(
            x_ref.at[:, pl.ds(slot * PEERS, PEERS), :], x_in.at[slot], in_sem.at[slot]
        ).wait()
        regroup(slot, slice(dim, 3 * dim), kv_out)
        if slot == 0:
            pl.semaphore_wait(barrier, len(OFFSETS))
        for d, f in OFFSETS:
            remote("kv", slot, d, f).start()
        own("kv", slot).start()
        regroup(slot, slice(0, dim), q_out)
        for d, f in OFFSETS:
            remote("q", slot, d, f).start()
        own("q", slot).start()

    exponent_scale = math.log2(math.e) / math.sqrt(dim)
    ones = jnp.ones((2 * dim, dim), jnp.bfloat16)
    step = 2 * dim

    def attend(slot, chip):
        rows = pl.ds(pl.multiple_of(chip * pair, pair), pair)
        biases = jnp.concatenate(
            [
                jnp.broadcast_to(bias[slot, pl.ds(chip * CORES + i, 1), :], (tokens, dim))
                for i in range(CORES)
            ],
            axis=0,
        )
        queries = jnp.concatenate([q_got[slot, rows, :], biases.astype(jnp.bfloat16)], axis=1)
        largest = None
        for start in range(0, keys, step):
            part = slice(start, start + step)
            key_part = jnp.concatenate([kv_got[slot, part, 0:dim], tile_of_key[part, :]], axis=1)
            found = lax.dot_general(
                queries, key_part, (((1,), (1,)), ((), ())), preferred_element_type=jnp.float32
            )
            scores[:, part] = found
            higher = jnp.maximum(found[:, 0:dim], found[:, dim:step])
            largest = higher if largest is None else jnp.maximum(largest, higher)
        row_max = jnp.max(largest, axis=1, keepdims=True)
        total = jnp.zeros((pair, 2 * dim), jnp.float32)
        for start in range(0, keys, step):
            part = slice(start, start + step)
            weights = jnp.exp2((scores[:, part] - row_max) * exponent_scale).astype(jnp.bfloat16)
            values = jnp.concatenate([kv_got[slot, part, dim : 2 * dim], ones], axis=1)
            total += jnp.dot(weights, values, preferred_element_type=jnp.float32)
        o_out[slot, rows, :] = (total[:, 0:dim] / total[:, dim : 2 * dim]).astype(jnp.bfloat16)

    for slot in range(slots):
        with jax.named_scope("wait_kv"):
            own("kv", slot).wait()
            for d, f in OFFSETS:
                remote("kv", slot, d, f).wait_recv()
        own("q", slot).wait()
        remote("q", slot, 0, 1).wait_recv()
        attend(slot, y)
        own("o", slot).start()
        remote("o", slot, 0, 1).start()

        def turn(number, carry, slot=slot):
            distance = (number + 2) // 2
            d = jnp.where(number % 2 == 0, distance, CHIPS - distance)
            for f in range(CORES):
                remote("q", slot, CHIPS - d, f).wait_recv()
            attend(slot, lax.rem(y + d, CHIPS))
            for f in range(CORES):
                remote("o", slot, d, f).start()
            return carry

        with jax.named_scope("attend"):
            lax.fori_loop(0, CHIPS - 1, turn, 0)

    with jax.named_scope("wait_last"):
        for slot in range(slots):
            own("o", slot).wait()
            for d, f in OFFSETS:
                remote("o", slot, d, f).wait_recv()
                for kind in ("kv", "q", "o"):
                    remote(kind, slot, d, f).wait_send()


def body(projections, tile_mask):
    tokens, heads, width = projections.shape
    dim = width // 3
    slots = heads // PEERS
    keys = tokens * PEERS
    return pl.pallas_call(
        kernel,
        out_shape=jax.ShapeDtypeStruct((tokens, heads * dim), jnp.bfloat16),
        in_specs=[pl.BlockSpec(memory_space=pl.ANY)] * 2,
        out_specs=pl.BlockSpec(memory_space=pl.ANY),
        scratch_shapes=[
            pltpu.VMEM((slots, tokens, PEERS, width), jnp.bfloat16),
            pltpu.VMEM((slots, PEERS, PEERS), jnp.int32),
            pltpu.VMEM((slots, PEERS, tokens, 2 * dim), jnp.bfloat16),
            pltpu.VMEM((slots, PEERS, tokens, dim), jnp.bfloat16),
            pltpu.VMEM((slots, keys, 2 * dim), jnp.bfloat16),
            pltpu.VMEM((slots, keys, dim), jnp.bfloat16),
            pltpu.VMEM((slots, keys, dim), jnp.bfloat16),
            pltpu.VMEM((keys, dim), jnp.bfloat16),
            pltpu.VMEM((slots, PEERS, dim), jnp.float32),
            pltpu.VMEM((CORES * tokens, keys), jnp.float32),
            pltpu.SemaphoreType.DMA((slots,)),
            pltpu.SemaphoreType.DMA((slots,)),
            pltpu.SemaphoreType.DMA((3 * slots,)),
            pltpu.SemaphoreType.DMA((3 * slots, PEERS)),
            pltpu.SemaphoreType.DMA((3 * slots, PEERS)),
        ],
        compiler_params=pltpu.CompilerParams(
            collective_id=0, has_side_effects=True, vmem_limit_bytes=48 << 20
        ),
    )(projections, tile_mask)


def solution(mesh):
    return jax.shard_map(
        body,
        mesh=mesh,
        in_specs=(P(("clip", "seq", "tp"), None, None), P("clip", None, None)),
        out_specs=P(("clip", "seq", "tp"), None),
        check_vma=False,
    )
```

time: 437 us -> 110 us (0.25)
  matrix products: 120 us -> 0 us
  Pallas kernels: 0 us -> 106 us
  loops' own time: 102 us -> 0 us
  local copies, waits for them, and re-layouts: 64.6 us -> 3.92 us
  waiting for transfers between devices: 58.6 us -> 0 us
  blocking collectives: 42.1 us -> 0 us
  other arithmetic: 31.5 us -> 0 us
  starting transfers between devices: 11.2 us -> 0 us
    dot_general x64 -> x0, matrix products: 120 us -> none  [the longest x31 77 us: advance(): jnp.dot(expo.astype(jnp.bfloat16), key_values[:, head_dim:], preferred_el...]
    pallas_call x0 -> x1, Pallas kernels: none -> 106 us  [body(): pl.pallas_call(kernel, out_shape=jax.ShapeDtypeStruct((tokens, heads * di...]
    another operation x2 -> x0, loops' own time: 102 us -> none  [head_attention(): lax.fori_loop(0, active_count, advance, start_state)]
    all_to_all x1 -> x0, waiting for transfers between devices: 58.6 us -> none  [body(): lax.all_to_all(joined, ('seq', 'tp'), split_axis=0, concat_axis=2, tiled=...]
    all_to_all x1 -> x0, blocking collectives: 42.1 us -> none  [body(): lax.all_to_all(finished, ('seq', 'tp'), split_axis=2, concat_axis=0, tile...]
    while x124 -> x0, local copies, waits for them, and re-layouts: 23.6 us -> none
    dynamic_slice x32 -> x0, local copies, waits for them, and re-layouts: 18.7 us -> none  [the longest x31 18.6 us: advance(): pair_index = pair_order[turn_index]]
    dynamic_update_slice x62 -> x0, other arithmetic: 11.6 us -> none  [the longest x31 5.91 us: advance(): row_max = lax.dynamic_update_slice_in_dim(row_max, new_max, query_start, 0)]
  transfers between devices with their start and end apart: 1 -> 0, of which waited for: 1 -> 0; matrix products, arithmetic and copies ran while one was open for 2% -> 0% of each run, Pallas kernels for 0% -> 0%
where the time goes in v1:
time: 110 us
  Pallas kernels  106 us (96%)
  local copies, waits for them, and re-layouts  3.92 us (4%)
    pallas_call x1, Pallas kernels, body(): pl.pallas_call(kernel, out_shape=jax.ShapeDtypeStruct((tokens, heads * di...  106 us
    unnamed x4, local copies, waits for them, and re-layouts  3.92 us

profile of v1, /device:TPU:1, one launch (start us, length us, event | category | flops | bytes accessed | tf_op | source)
XLA Modules:
  0.0 109.8 jit_solution(622421751203358087)
XLA Ops:
  0.0 1.1 copy.3.mask_ref
  1.1 0.0 copy-start
  1.1 1.9 %copy-done = bf16[128,32,384]{2,1,0:T(8,128)(2,1)S(1)} copy-done((bf16[128,32,384]{2,1,0:T(8,128)(2,1)S(1)}, bf16[128,32,384]{2,1,0:T(8,128)(2,1)}, u32[]{:S(2)}) %copy-start) | copy-done | bytes 3145752
  3.0 105.9 %shard_map.28 = bf16[128,4096]{1,0:T(8,128)(2,1)S(1)} custom-call(bf16[128,32,384]{2,1,0:T(8,128)(2,1)S(1)} %copy-done, s32[32,16,16]{2,1,0:T(8,128)S(1)} %copy.3.mask_ref), custom_call_target="tpu_custom_call" | custom-call | tf_op jit(solution)/shard_map/pallas_call | solution.py:209
  108.9 1.0 copy.5
Async XLA Ops:
  1.1 1.9 %copy-start = (bf16[128,32,384]{2,1,0:T(8,128)(2,1)S(1)}, bf16[128,32,384]{2,1,0:T(8,128)(2,1)}, u32[]{:S(2)}) copy-start(bf16[128,32,384]{2,1,0:T(8,128)(2,1)} %x_ref.1) | copy-start | bytes 9437188

commit v2 on v1

v2 whole, which is shorter than its diff:
```python
import functools
import math

import jax
import jax.numpy as jnp
from jax import lax
from jax.experimental import pallas as pl
from jax.experimental.pallas import tpu as pltpu
from jax.sharding import PartitionSpec as P

MESH = pl.DeviceIdType.MESH
NEGATIVE_FILL = -1e30
CHIPS = 8
CORES = 2
PEERS = CHIPS * CORES
REACH = (1, 7, 2, 6, 3, 5, 4)
OFFSETS = tuple((d, f) for d in REACH for f in range(CORES)) + ((0, 1),)


def kernel(
    x_ref,
    mask_ref,
    out_ref,
    x_in,
    mask_in,
    qkv_out,
    qkv_got,
    o_out,
    tile_of_key,
    bias,
    scores,
    in_sem,
    mask_sem,
    own_sem,
    send_sem,
    recv_sem,
):
    y = lax.axis_index("seq")
    core = lax.axis_index("tp")
    me = y * CORES + core
    tokens, _, width = x_ref.shape
    slots = x_in.shape[0]
    dim = width // 3
    pair = CORES * tokens
    keys = qkv_got.shape[1]

    x_copies = [
        pltpu.make_async_copy(
            x_ref.at[:, pl.ds(slot * PEERS, PEERS), :], x_in.at[slot], in_sem.at[slot]
        )
        for slot in range(slots)
    ]
    x_copies[0].start()

    def peer(d, f):
        return {"seq": lax.rem(y + d, CHIPS), "tp": lax.rem(core + f, CORES)}

    def index_of(d, f):
        return lax.rem(y + d, CHIPS) * CORES + lax.rem(core + f, CORES)

    barrier = pltpu.get_barrier_semaphore()
    for d, f in OFFSETS:
        pl.semaphore_signal(barrier, inc=1, device_id=peer(d, f), device_id_type=MESH)
    for copy in x_copies[1:]:
        copy.start()
    mask_copy = pltpu.make_async_copy(mask_ref, mask_in, mask_sem)
    mask_copy.start()

    def rows_of(device):
        return pl.ds(pl.multiple_of(device * tokens, tokens), tokens)

    def ends(kind, slot, to):
        if kind == "qkv":
            return qkv_out.at[slot, to], qkv_got.at[slot, rows_of(me)], slot
        columns = pl.ds(pl.multiple_of((slot * PEERS + me) * dim, dim), dim)
        return o_out.at[slot, rows_of(to)], out_ref.at[:, columns], slots + slot

    def remote(kind, slot, d, f):
        src, dst, row = ends(kind, slot, index_of(d, f))
        number = d * CORES + f
        return pltpu.make_async_remote_copy(
            src_ref=src,
            dst_ref=dst,
            send_sem=send_sem.at[row, number],
            recv_sem=recv_sem.at[row, number],
            device_id=peer(d, f),
            device_id_type=MESH,
        )

    def own(kind, slot):
        src, dst, row = ends(kind, slot, me)
        return pltpu.make_async_copy(src, dst, own_sem.at[row])

    side = PEERS * PEERS
    to_row = lax.broadcasted_iota(jnp.int32, (side, side), 0)
    from_row = lax.broadcasted_iota(jnp.int32, (side, side), 1)
    swap = (from_row == (to_row % PEERS) * PEERS + to_row // PEERS).astype(jnp.bfloat16)

    def regroup(slot):
        for start in range(0, tokens, PEERS):
            block = x_in[slot, start : start + PEERS].reshape(side, width)
            swapped = jnp.dot(swap, block, preferred_element_type=jnp.float32)
            qkv_out[slot, :, start : start + PEERS, :] = swapped.astype(jnp.bfloat16).reshape(
                PEERS, PEERS, width
            )

    for slot in range(slots):
        x_copies[slot].wait()
        regroup(slot)
        if slot == 0:
            pl.semaphore_wait(barrier, len(OFFSETS))
        for d, f in OFFSETS:
            remote("qkv", slot, d, f).start()
        own("qkv", slot).start()

    tile_of_key[...] = (
        lax.broadcasted_iota(jnp.int32, tile_of_key.shape, 0) // tokens
        == lax.broadcasted_iota(jnp.int32, tile_of_key.shape, 1)
    ).astype(jnp.bfloat16)
    bias[...] = jnp.zeros_like(bias)
    mask_copy.wait()
    heads = mask_in.shape[2]
    my_head = lax.broadcasted_iota(jnp.int32, (8, heads), 0) * PEERS + me
    pick = (my_head == lax.broadcasted_iota(jnp.int32, (8, heads), 1)).astype(jnp.bfloat16)
    for tile in range(PEERS):
        allowed = lax.dot_general(
            pick,
            (mask_in[tile] > 0).astype(jnp.bfloat16),
            (((1,), (1,)), ((), ())),
            preferred_element_type=jnp.float32,
        )
        bias[tile, :, 0:PEERS] = jnp.where(allowed > 0.5, 0.0, NEGATIVE_FILL)

    exponent_scale = math.log2(math.e) / math.sqrt(dim)
    ones = jnp.ones((2 * dim, dim), jnp.bfloat16)
    step = 2 * dim

    def attend(slot, chip):
        rows = pl.ds(pl.multiple_of(chip * pair, pair), pair)
        biases = jnp.concatenate(
            [
                jnp.broadcast_to(bias[chip * CORES + i, slot : slot + 1, :], (tokens, dim))
                for i in range(CORES)
            ],
            axis=0,
        )
        queries = jnp.concatenate([qkv_got[slot, rows, 0:dim], biases.astype(jnp.bfloat16)], axis=1)
        largest = None
        for start in range(0, keys, step):
            part = slice(start, start + step)
            key_part = jnp.concatenate([qkv_got[slot, part, dim : 2 * dim], tile_of_key[part, :]], axis=1)
            found = lax.dot_general(
                queries, key_part, (((1,), (1,)), ((), ())), preferred_element_type=jnp.float32
            )
            scores[:, part] = found
            higher = jnp.maximum(found[:, 0:dim], found[:, dim:step])
            largest = higher if largest is None else jnp.maximum(largest, higher)
        row_max = jnp.max(largest, axis=1, keepdims=True)
        total = jnp.zeros((pair, 2 * dim), jnp.float32)
        for start in range(0, keys, step):
            part = slice(start, start + step)
            weights = jnp.exp2((scores[:, part] - row_max) * exponent_scale).astype(jnp.bfloat16)
            values = jnp.concatenate([qkv_got[slot, part, 2 * dim : 3 * dim], ones], axis=1)
            total += jnp.dot(weights, values, preferred_element_type=jnp.float32)
        o_out[slot, rows, :] = (total[:, 0:dim] / total[:, dim : 2 * dim]).astype(jnp.bfloat16)

    for slot in range(slots):
        own("qkv", slot).wait()
        for d, f in OFFSETS:
            remote("qkv", slot, d, f).wait_recv()
        attend(slot, y)
        own("o", slot).start()
        remote("o", slot, 0, 1).start()

        def turn(number, carry, slot=slot):
            distance = (number + 2) // 2
            d = jnp.where(number % 2 == 0, distance, CHIPS - distance)
            attend(slot, lax.rem(y + d, CHIPS))
            for f in range(CORES):
                remote("o", slot, d, f).start()
            return carry

        lax.fori_loop(0, CHIPS - 1, turn, 0)

    for kind in ("qkv", "o"):
        for slot in range(slots):
            if kind == "o":
                own("o", slot).wait()
            for d, f in OFFSETS:
                remote(kind, slot, d, f).wait_send()
    for slot in range(slots):
        for d, f in OFFSETS:
            remote("o", slot, d, f).wait_recv()


def body(projections, tile_mask):
    tokens, heads, width = projections.shape
    dim = width // 3
    slots = heads // PEERS
    keys = tokens * PEERS
    return pl.pallas_call(
        kernel,
        out_shape=jax.ShapeDtypeStruct((tokens, heads * dim), jnp.bfloat16),
        in_specs=[pl.BlockSpec(memory_space=pltpu.HBM)] * 2,
        out_specs=pl.BlockSpec(memory_space=pl.ANY),
        scratch_shapes=[
            pltpu.VMEM((slots, tokens, PEERS, width), jnp.bfloat16),
            pltpu.VMEM((PEERS, PEERS, heads), jnp.int32),
            pltpu.VMEM((slots, PEERS, tokens, width), jnp.bfloat16),
            pltpu.VMEM((slots, keys, width), jnp.bfloat16),
            pltpu.VMEM((slots, keys, dim), jnp.bfloat16),
            pltpu.VMEM((keys, dim), jnp.bfloat16),
            pltpu.VMEM((PEERS, 8, dim), jnp.float32),
            pltpu.VMEM((CORES * tokens, keys), jnp.float32),
            pltpu.SemaphoreType.DMA((slots,)),
            pltpu.SemaphoreType.DMA,
            pltpu.SemaphoreType.DMA((2 * slots,)),
            pltpu.SemaphoreType.DMA((2 * slots, PEERS)),
            pltpu.SemaphoreType.DMA((2 * slots, PEERS)),
        ],
        compiler_params=pltpu.CompilerParams(
            collective_id=0, has_side_effects=True, vmem_limit_bytes=48 << 20
        ),
    )(
        pltpu.with_memory_space_constraint(projections, pltpu.HBM),
        pltpu.with_memory_space_constraint(jnp.transpose(tile_mask, (1, 2, 0)), pltpu.HBM),
    )


def solution(mesh):
    return jax.shard_map(
        body,
        mesh=mesh,
        in_specs=(P(("clip", "seq", "tp"), None, None), P("clip", None, None)),
        out_specs=P(("clip", "seq", "tp"), None),
        check_vma=False,
    )
```

time: 110 us -> 104 us (0.945)
  Pallas kernels: 106 us -> 103 us
  local copies, waits for them, and re-layouts: 3.92 us -> 0.97 us
    unnamed x4 -> x1, local copies, waits for them, and re-layouts: 3.92 us -> 0.97 us
    pallas_call x1, Pallas kernels: 106 us -> 103 us  [body(): pl.pallas_call(kernel, out_shape=jax.ShapeDtypeStruct((tokens, heads * di...]
where the time goes in v2:
time: 104 us
  Pallas kernels  103 us (99%)
    pallas_call x1, Pallas kernels, body(): pl.pallas_call(kernel, out_shape=jax.ShapeDtypeStruct((tokens, heads * di...  103 us

profile of v2, /device:TPU:1, one launch (start us, length us, event | category | flops | bytes accessed | tf_op | source)
XLA Modules:
  0.0 104.2 jit_solution(17526239337397228065)
XLA Ops:
  0.0 103.2 %shard_map.28 = bf16[128,4096]{1,0:T(8,128)(2,1)S(1)} custom-call(bf16[128,32,384]{2,1,0:T(8,128)(2,1)} %x_ref.1, s32[16,16,32]{2,1,0:T(8,128)} %bitcast.1), custom_call_target="tpu_custom_call" | custom-call | tf_op jit(solution)/shard_map/pallas_call | solution.py:201
  103.2 1.0 copy.4

commit v3 on v2

--- a/solution.py
+++ b/solution.py
@@ -13,6 +13,7 @@
 CHIPS = 8
 CORES = 2
 PEERS = CHIPS * CORES
+LAST = 0
 REACH = (1, 7, 2, 6, 3, 5, 4)
 OFFSETS = tuple((d, f) for d in REACH for f in range(CORES)) + ((0, 1),)
 
@@ -34,6 +35,7 @@
     own_sem,
     send_sem,
     recv_sem,
+    ready_sem,
 ):
     y = lax.axis_index("seq")
     core = lax.axis_index("tp")
@@ -59,8 +61,12 @@
         return lax.rem(y + d, CHIPS) * CORES + lax.rem(core + f, CORES)
 
     barrier = pltpu.get_barrier_semaphore()
-    for d, f in OFFSETS:
-        pl.semaphore_signal(barrier, inc=1, device_id=peer(d, f), device_id_type=MESH)
+
+    @pl.when(me != LAST)
+    def _():
+        for d, f in OFFSETS:
+            pl.semaphore_signal(barrier, inc=1, device_id=peer(d, f), device_id_type=MESH)
+
     for copy in x_copies[1:]:
         copy.start()
     mask_copy = pltpu.make_async_copy(mask_ref, mask_in, mask_sem)
@@ -104,14 +110,39 @@
                 PEERS, PEERS, width
             )
 
-    for slot in range(slots):
-        x_copies[slot].wait()
-        regroup(slot)
-        if slot == 0:
-            pl.semaphore_wait(barrier, len(OFFSETS))
-        for d, f in OFFSETS:
-            remote("qkv", slot, d, f).start()
-        own("qkv", slot).start()
+    x_copies[0].wait()
+    regroup(0)
+
+    @pl.when(me != LAST)
+    def _():
+        pl.semaphore_wait(barrier, len(OFFSETS) - 1)
+
+    @pl.when(me == LAST)
+    def _():
+        pl.semaphore_wait(barrier, len(OFFSETS))
+        for d, f in OFFSETS:
+            pl.semaphore_signal(ready_sem, inc=1, device_id=peer(d, f), device_id_type=MESH)
+
+    for d, f in OFFSETS:
+
+        @pl.when(index_of(d, f) != LAST)
+        def _(d=d, f=f):
+            remote("qkv", 0, d, f).start()
+
+    own("qkv", 0).start()
+    x_copies[1].wait()
+    regroup(1)
+
+    @pl.when(me != LAST)
+    def _():
+        pl.semaphore_wait(ready_sem, 1)
+        d = lax.rem(LAST // CORES + CHIPS - y, CHIPS)
+        f = lax.rem(LAST % CORES + CORES - core, CORES)
+        remote("qkv", 0, d, f).start()
+
+    for d, f in OFFSETS:
+        remote("qkv", 1, d, f).start()
+    own("qkv", 1).start()
 
     tile_of_key[...] = (
         lax.broadcasted_iota(jnp.int32, tile_of_key.shape, 0) // tokens
@@ -217,6 +248,7 @@
             pltpu.SemaphoreType.DMA((2 * slots,)),
             pltpu.SemaphoreType.DMA((2 * slots, PEERS)),
             pltpu.SemaphoreType.DMA((2 * slots, PEERS)),
+            pltpu.SemaphoreType.REGULAR,
         ],
         compiler_params=pltpu.CompilerParams(
             collective_id=0, has_side_effects=True, vmem_limit_bytes=48 << 20

time: 104 us -> 101 us (0.971); the launches traced: 104 us -> 100 us
  Pallas kernels: 103 us -> 99 us
    pallas_call x1, Pallas kernels: 103 us -> 99 us  [body(): pl.pallas_call(kernel, out_shape=jax.ShapeDtypeStruct((tokens, heads * di...]
where the time goes in v3:
time: 101 us; the launch traced here: 100 us
  Pallas kernels  99 us (98%)
    pallas_call x1, Pallas kernels, body(): pl.pallas_call(kernel, out_shape=jax.ShapeDtypeStruct((tokens, heads * di...  99 us

profile of v3, /device:TPU:1, one launch (start us, length us, event | category | flops | bytes accessed | tf_op | source)
XLA Modules:
  0.0 100.0 jit_solution(83234048225070867)
XLA Ops:
  0.0 99.0 %shard_map.28 = bf16[128,4096]{1,0:T(8,128)(2,1)S(1)} custom-call(bf16[128,32,384]{2,1,0:T(8,128)(2,1)} %x_ref.1, s32[16,16,32]{2,1,0:T(8,128)} %bitcast.1), custom_call_target="tpu_custom_call" | custom-call | tf_op jit(solution)/shard_map/pallas_call | solution.py:232
  99.0 1.0 copy.4

commit v4 on v3

--- a/solution.py
+++ b/solution.py
@@ -79,23 +79,38 @@
         if kind == "qkv":
             return qkv_out.at[slot, to], qkv_got.at[slot, rows_of(me)], slot
         columns = pl.ds(pl.multiple_of((slot * PEERS + me) * dim, dim), dim)
-        return o_out.at[slot, rows_of(to)], out_ref.at[:, columns], slots + slot
+        return o_out.at[slot, rows_of(to)], out_ref.at[:, columns], slots
 
     def remote(kind, slot, d, f):
-        src, dst, row = ends(kind, slot, index_of(d, f))
-        number = d * CORES + f
+        src, dst, number = ends(kind, slot, index_of(d, f))
         return pltpu.make_async_remote_copy(
             src_ref=src,
             dst_ref=dst,
-            send_sem=send_sem.at[row, number],
-            recv_sem=recv_sem.at[row, number],
+            send_sem=send_sem.at[number],
+            recv_sem=recv_sem.at[number],
             device_id=peer(d, f),
             device_id_type=MESH,
         )
 
+    def all_of(kind, slot=0):
+        others = PEERS - 1
+        if kind == "qkv":
+            src, dst, number = qkv_out.at[slot, 0:others], qkv_got.at[slot, 0 : others * tokens], slot
+        else:
+            src = o_out.at[:, 0 : others * tokens]
+            dst, number = out_ref.at[:, 0 : slots * others * dim], slots
+        return pltpu.make_async_remote_copy(
+            src_ref=src,
+            dst_ref=dst,
+            send_sem=send_sem.at[number],
+            recv_sem=recv_sem.at[number],
+            device_id=peer(0, 1),
+            device_id_type=MESH,
+        )
+
     def own(kind, slot):
-        src, dst, row = ends(kind, slot, me)
-        return pltpu.make_async_copy(src, dst, own_sem.at[row])
+        src, dst, number = ends(kind, slot, me)
+        return pltpu.make_async_copy(src, dst, own_sem.at[number + slot if kind == "o" else number])
 
     side = PEERS * PEERS
     to_row = lax.broadcasted_iota(jnp.int32, (side, side), 0)
@@ -197,8 +212,7 @@
 
     for slot in range(slots):
         own("qkv", slot).wait()
-        for d, f in OFFSETS:
-            remote("qkv", slot, d, f).wait_recv()
+        all_of("qkv", slot).wait_recv()
         attend(slot, y)
         own("o", slot).start()
         remote("o", slot, 0, 1).start()
@@ -213,15 +227,11 @@
 
         lax.fori_loop(0, CHIPS - 1, turn, 0)
 
-    for kind in ("qkv", "o"):
-        for slot in range(slots):
-            if kind == "o":
-                own("o", slot).wait()
-            for d, f in OFFSETS:
-                remote(kind, slot, d, f).wait_send()
     for slot in range(slots):
-        for d, f in OFFSETS:
-            remote("o", slot, d, f).wait_recv()
+        all_of("qkv", slot).wait_send()
+        own("o", slot).wait()
+    all_of("o").wait_send()
+    all_of("o").wait_recv()
 
 
 def body(projections, tile_mask):
@@ -246,8 +256,8 @@
             pltpu.SemaphoreType.DMA((slots,)),
             pltpu.SemaphoreType.DMA,
             pltpu.SemaphoreType.DMA((2 * slots,)),
-            pltpu.SemaphoreType.DMA((2 * slots, PEERS)),
-            pltpu.SemaphoreType.DMA((2 * slots, PEERS)),
+            pltpu.SemaphoreType.DMA((slots + 1,)),
+            pltpu.SemaphoreType.DMA((slots + 1,)),
             pltpu.SemaphoreType.REGULAR,
         ],
         compiler_params=pltpu.CompilerParams(

time: 101 us -> 100 us (0.990)
  Pallas kernels: 99 us -> 97.9 us
    pallas_call x1, Pallas kernels: 99 us -> 97.9 us  [body(): pl.pallas_call(kernel, out_shape=jax.ShapeDtypeStruct((tokens, heads * di...]
where the time goes in v4:
time: 100 us; the launch traced here: 98.9 us
  Pallas kernels  97.9 us (98%)
    pallas_call x1, Pallas kernels, body(): pl.pallas_call(kernel, out_shape=jax.ShapeDtypeStruct((tokens, heads * di...  97.9 us

profile of v4, /device:TPU:1, one launch (start us, length us, event | category | flops | bytes accessed | tf_op | source)
XLA Modules:
  0.0 98.9 jit_solution(3193317556932957933)
XLA Ops:
  0.0 97.9 %shard_map.28 = bf16[128,4096]{1,0:T(8,128)(2,1)S(1)} custom-call(bf16[128,32,384]{2,1,0:T(8,128)(2,1)} %x_ref.1, s32[16,16,32]{2,1,0:T(8,128)} %bitcast.1), custom_call_target="tpu_custom_call" | custom-call | tf_op jit(solution)/shard_map/pallas_call | solution.py:242
  97.9 1.0 copy.4

commit v5 on v4

--- a/solution.py
+++ b/solution.py
@@ -13,7 +13,8 @@
 CHIPS = 8
 CORES = 2
 PEERS = CHIPS * CORES
-LAST = 0
+LATE = (0, 8, 9, 10, 11)
+TELLS = ((1, 0), (6, 8), (7, 9), (12, 10), (13, 11))
 REACH = (1, 7, 2, 6, 3, 5, 4)
 OFFSETS = tuple((d, f) for d in REACH for f in range(CORES)) + ((0, 1),)
 
@@ -60,9 +61,14 @@
     def index_of(d, f):
         return lax.rem(y + d, CHIPS) * CORES + lax.rem(core + f, CORES)
 
+    def is_late(device):
+        return functools.reduce(jnp.logical_or, [device == late for late in LATE])
+
     barrier = pltpu.get_barrier_semaphore()
-
-    @pl.when(me != LAST)
+    late = is_late(me)
+    early = jnp.logical_not(late)
+
+    @pl.when(early)
     def _():
         for d, f in OFFSETS:
             pl.semaphore_signal(barrier, inc=1, device_id=peer(d, f), device_id_type=MESH)
@@ -128,19 +134,22 @@
     x_copies[0].wait()
     regroup(0)
 
-    @pl.when(me != LAST)
-    def _():
-        pl.semaphore_wait(barrier, len(OFFSETS) - 1)
-
-    @pl.when(me == LAST)
-    def _():
-        pl.semaphore_wait(barrier, len(OFFSETS))
+    @pl.when(early)
+    def _():
+        pl.semaphore_wait(barrier, PEERS - len(LATE) - 1)
+
+    @pl.when(late)
+    def _():
+        pl.semaphore_wait(barrier, PEERS - len(LATE))
         for d, f in OFFSETS:
-            pl.semaphore_signal(ready_sem, inc=1, device_id=peer(d, f), device_id_type=MESH)
+
+            @pl.when(jnp.logical_not(is_late(index_of(d, f))))
+            def _(d=d, f=f):
+                pl.semaphore_signal(ready_sem, inc=1, device_id=peer(d, f), device_id_type=MESH)
 
     for d, f in OFFSETS:
 
-        @pl.when(index_of(d, f) != LAST)
+        @pl.when(jnp.logical_not(is_late(index_of(d, f))))
         def _(d=d, f=f):
             remote("qkv", 0, d, f).start()
 
@@ -148,12 +157,29 @@
     x_copies[1].wait()
     regroup(1)
 
-    @pl.when(me != LAST)
+    @pl.when(early)
+    def _():
+        pl.semaphore_wait(ready_sem, len(LATE))
+        for teller, told in TELLS:
+
+            @pl.when(me == teller)
+            def _(told=told):
+                pl.semaphore_signal(
+                    ready_sem,
+                    inc=1,
+                    device_id={"seq": told // CORES, "tp": told % CORES},
+                    device_id_type=MESH,
+                )
+
+    @pl.when(late)
     def _():
         pl.semaphore_wait(ready_sem, 1)
-        d = lax.rem(LAST // CORES + CHIPS - y, CHIPS)
-        f = lax.rem(LAST % CORES + CORES - core, CORES)
-        remote("qkv", 0, d, f).start()
+
+    for d, f in OFFSETS:
+
+        @pl.when(is_late(index_of(d, f)))
+        def _(d=d, f=f):
+            remote("qkv", 0, d, f).start()
 
     for d, f in OFFSETS:
         remote("qkv", 1, d, f).start()
@@ -218,7 +244,7 @@
         remote("o", slot, 0, 1).start()
 
         def turn(number, carry, slot=slot):
-            distance = (number + 2) // 2
+            distance = (CHIPS - number) // 2
             d = jnp.where(number % 2 == 0, distance, CHIPS - distance)
             attend(slot, lax.rem(y + d, CHIPS))
             for f in range(CORES):

time: 100 us -> 99.9 us (level); the launches traced: 98.9 us -> 99.8 us
  no operation moved by 1% of the time
where the time goes in v5:
time: 99.9 us; the launch traced here: 99.8 us
  Pallas kernels  98.8 us (99%)
    pallas_call x1, Pallas kernels, body(): pl.pallas_call(kernel, out_shape=jax.ShapeDtypeStruct((tokens, heads * di...  98.8 us

profile of v5, /device:TPU:1, one launch (start us, length us, event | category | flops | bytes accessed | tf_op | source)
XLA Modules:
  0.0 99.8 jit_solution(4712160634262320064)
XLA Ops:
  0.0 98.8 %shard_map.28 = bf16[128,4096]{1,0:T(8,128)(2,1)S(1)} custom-call(bf16[128,32,384]{2,1,0:T(8,128)(2,1)} %x_ref.1, s32[16,16,32]{2,1,0:T(8,128)} %bitcast.1), custom_call_target="tpu_custom_call" | custom-call | tf_op jit(solution)/shard_map/pallas_call | solution.py:268
  98.8 1.0 copy.4

commit v6 on v5

--- a/solution.py
+++ b/solution.py
@@ -16,6 +16,7 @@
 LATE = (0, 8, 9, 10, 11)
 TELLS = ((1, 0), (6, 8), (7, 9), (12, 10), (13, 11))
 REACH = (1, 7, 2, 6, 3, 5, 4)
+SECOND = tuple((d, f) for d in (3, 5, 4, 2, 6, 1, 7) for f in range(CORES)) + ((0, 1),)
 OFFSETS = tuple((d, f) for d in REACH for f in range(CORES)) + ((0, 1),)
 
 
@@ -181,7 +182,7 @@
         def _(d=d, f=f):
             remote("qkv", 0, d, f).start()
 
-    for d, f in OFFSETS:
+    for d, f in SECOND:
         remote("qkv", 1, d, f).start()
     own("qkv", 1).start()
 

time: 99.9 us -> 99.8 us (level)
  no operation moved by 1% of the time
where the time goes in v6:
time: 99.8 us; the launch traced here: 99.7 us
  Pallas kernels  98.7 us (99%)
    pallas_call x1, Pallas kernels, body(): pl.pallas_call(kernel, out_shape=jax.ShapeDtypeStruct((tokens, heads * di...  98.7 us

profile of v6, /device:TPU:1, one launch (start us, length us, event | category | flops | bytes accessed | tf_op | source)
XLA Modules:
  0.0 99.7 jit_solution(2989404484651643359)
XLA Ops:
  0.0 98.7 %shard_map.28 = bf16[128,4096]{1,0:T(8,128)(2,1)S(1)} custom-call(bf16[128,32,384]{2,1,0:T(8,128)(2,1)} %x_ref.1, s32[16,16,32]{2,1,0:T(8,128)} %bitcast.1), custom_call_target="tpu_custom_call" | custom-call | tf_op jit(solution)/shard_map/pallas_call | solution.py:269
  98.7 1.0 copy.4

commit v7 on v6

--- a/solution.py
+++ b/solution.py
@@ -79,6 +79,15 @@
     mask_copy = pltpu.make_async_copy(mask_ref, mask_in, mask_sem)
     mask_copy.start()
 
+    @pl.when(late)
+    def _():
+        pl.semaphore_wait(barrier, PEERS - len(LATE))
+        for d, f in OFFSETS:
+
+            @pl.when(jnp.logical_not(is_late(index_of(d, f))))
+            def _(d=d, f=f):
+                pl.semaphore_signal(ready_sem, inc=1, device_id=peer(d, f), device_id_type=MESH)
+
     def rows_of(device):
         return pl.ds(pl.multiple_of(device * tokens, tokens), tokens)
 
@@ -138,15 +147,6 @@
     @pl.when(early)
     def _():
         pl.semaphore_wait(barrier, PEERS - len(LATE) - 1)
-
-    @pl.when(late)
-    def _():
-        pl.semaphore_wait(barrier, PEERS - len(LATE))
-        for d, f in OFFSETS:
-
-            @pl.when(jnp.logical_not(is_late(index_of(d, f))))
-            def _(d=d, f=f):
-                pl.semaphore_signal(ready_sem, inc=1, device_id=peer(d, f), device_id_type=MESH)
 
     for d, f in OFFSETS:
 

time: 99.8 us -> 99.7 us (level)
  no operation moved by 1% of the time
where the time goes in v7:
time: 99.7 us; the launch traced here: 99.6 us
  Pallas kernels  98.6 us (99%)
    pallas_call x1, Pallas kernels, body(): pl.pallas_call(kernel, out_shape=jax.ShapeDtypeStruct((tokens, heads * di...  98.6 us

profile of v7, /device:TPU:1, one launch (start us, length us, event | category | flops | bytes accessed | tf_op | source)
XLA Modules:
  0.0 99.6 jit_solution(2047935725407838012)
XLA Ops:
  0.0 98.6 %shard_map.28 = bf16[128,4096]{1,0:T(8,128)(2,1)S(1)} custom-call(bf16[128,32,384]{2,1,0:T(8,128)(2,1)} %x_ref.1, s32[16,16,32]{2,1,0:T(8,128)} %bitcast.1), custom_call_target="tpu_custom_call" | custom-call | tf_op jit(solution)/shard_map/pallas_call | solution.py:269
  98.6 1.0 copy.4
